TPU v7x, 32 devices: a whole 2x2x4 slice. The times are simulated.
32 devices in a mesh: row: 4 (over y, x), col: 8 (over z, core).
Axes of the slice: x: 2, y: 2, z: 4, core: 2. Of those that a mesh axis runs over, the one named last changes fastest.
Arguments:
- tiles: bfloat16 [256, 256, 256], P(('row', 'col')), may hold values from -0.09375 to 0.09375
- tile_rows: int32 [256], P(('row', 'col')), may hold values from 0 to 3, as said below
- tile_cols: int32 [256], P(('row', 'col')), may hold values from 0 to 1
- tile_count: int32 [32], P(('row', 'col')), may hold values from 0 to 8, as said below
- bounds: float32 [2], replicated, may hold values from -1 to 2, as said below
- vectors: float32 [4096, 128], P(('row', 'col')), may hold values from -6 to 6
Outputs:
- filtered: float32 [4096, 128], P(('row', 'col'))
- gram: float32 [128, 128], replicated
Inputs may be any that keep to these rules, and one draw needn't show every extreme that they name: `tile_rows`: within each device the first tile_count slots name distinct blocks with global block row I <= global block column J; the device's diagonal blocks (I = J) come first; every diagonal block of the Hamiltonian is stored; slots after the live ones hold valid indices but are not part of the matrix. `tile_count`: devices whose block rows all lie below their block columns have no live slot; some device has all 8 slots live. bounds[0] < -0.5 and bounds[1] > 1.0.
All inputs are finite; a program needn't handle non-finite values.
Results may differ from a plain program's by a relative error of at most 0.0037.
Values may be sent and summed in bfloat16 or wider, within the bound.
A program may use at most 64 MiB of HBM per device.

v0:
```python
import jax
import jax.numpy as jnp
from jax import lax
from jax.sharding import PartitionSpec as P

BLK_COL = 2


def spread(block, axis, holder):
    block = jnp.where(lax.axis_index(axis) == holder, block, jnp.zeros_like(block))
    return lax.psum(block, axis)


def on_device(tiles, tile_rows, tile_cols, tile_count, bounds, vectors):
    col_ratio = lax.axis_size("col") // lax.axis_size("row")
    col_index = lax.axis_index("col")
    row_index = lax.axis_index("row")
    root_row = col_index // col_ratio
    slot_total = tiles.shape[0]
    block_size = tiles.shape[1]
    share_rows = vectors.shape[0]
    width_vecs = vectors.shape[1]
    group_rows = share_rows * lax.axis_size("col")
    group_blocks = group_rows // block_size
    column_rows = BLK_COL * block_size
    total_rows = share_rows * lax.axis_size("row") * lax.axis_size("col")
    offset = col_index % col_ratio * column_rows
    live_mask = (jnp.arange(slot_total, dtype=jnp.int32) < tile_count[0]).astype(jnp.bfloat16)
    owner_flag = (row_index == root_row).astype(jnp.float32)
    center = (bounds[1] + bounds[0]) * 0.5
    halfwidth = (bounds[1] - bounds[0]) * 0.5

    def apply_hamiltonian(current_vec):
        vector_panel = current_vec.astype(jnp.bfloat16)
        row_panel = lax.all_gather(vector_panel, "col", axis=0, tiled=True)
        col_piece = lax.dynamic_slice_in_dim(row_panel, offset, column_rows, 0)
        col_panel = spread(col_piece, "row", root_row)
        row_input = row_panel.reshape(group_blocks, block_size, width_vecs)
        col_input = col_panel.reshape(BLK_COL, block_size, width_vecs)
        start_rows = jnp.zeros((group_blocks, block_size, width_vecs), jnp.float32)
        start_cols = jnp.zeros((BLK_COL, block_size, width_vecs), jnp.float32)
        masked_cols = col_input[tile_cols] * live_mask[:, None, None]
        masked_rows = row_input[tile_rows] * live_mask[:, None, None]
        forward = jnp.einsum("tab,tbk->tak", tiles, masked_cols, preferred_element_type=jnp.float32)
        backward = jnp.einsum(
            "tab,tak->tbk", tiles, masked_rows, preferred_element_type=jnp.float32
        )
        row_part = start_rows.at[tile_rows].add(forward)
        col_part = start_cols.at[tile_cols].add(backward)
        column_total = lax.psum(col_part, "row")
        row_part = row_part.reshape(group_rows, width_vecs)
        present = lax.dynamic_slice_in_dim(row_part, offset, column_rows, 0)
        updated = present + owner_flag * column_total.reshape(column_rows, width_vecs)
        row_part = lax.dynamic_update_slice_in_dim(row_part, updated, offset, 0)
        return lax.psum_scatter(row_part, "col", scatter_dimension=0, tiled=True)

    current_vec = (apply_hamiltonian(vectors) - center * vectors) / halfwidth
    image = apply_hamiltonian(current_vec)
    following = 2.0 * (image - center * current_vec) / halfwidth - vectors
    current_vec = following
    gram_local = lax.dot_general(
        current_vec,
        current_vec,
        (((0,), (0,)), ((), ())),
        precision=lax.Precision.HIGHEST,
        preferred_element_type=jnp.float32,
    )
    gram_total = lax.psum(gram_local, ("row", "col"))
    return (current_vec, gram_total / total_rows)


def solution(mesh):
    in_specs = (
        P(("row", "col"), None, None),
        P(("row", "col")),
        P(("row", "col")),
        P(("row", "col")),
        P(),
        P(("row", "col"), None),
    )
    out_specs = (P(("row", "col"), None), P())
    return jax.shard_map(
        on_device, mesh=mesh, in_specs=in_specs, out_specs=out_specs, check_vma=False
    )
```

profile of v0, /device:TPU:0, one launch (start us, length us, event | category | flops | bytes accessed | tf_op | source)
XLA Modules:
  0.0 413.3 jit_solution(1064199134010569408)
XLA Ops:
  7.2 0.9 convert_element_type.16
  8.2 15.9 %all_gather.6 = bf16[1024,128]{1,0:T(8,128)(2,1)S(1)} all-gather(bf16[128,128]{1,0:T(8,128)(2,1)S(1)} %convert_element_type.16), channel_id=1, replica_groups=mesh['row'=4,'col'=8] {'col'}, dimensions={0}, use_global_device_ids=true | all-gather | bytes 294912 | tf_op jit(solution)/shard_map/all_gather | solution.py:35
  24.0 0.7 dynamic-slice_select_fusion.1
  27.9 1.3 scatter_fusion.1
  29.2 0.7 copy-done.4
  30.0 37.9 %all-reduce.6.cloned.1.call-done = bf16[2,256,128]{2,1,0:T(8,128)(2,1)} async-done(((bf16[2,256,128]{2,1,0:T(8,128)(2,1)}), bf16[2,256,128]{2,1,0:T(8,128)(2,1)}) %all-reduce.6.cloned.1.call-update) | async-done | bytes 131088 | tf_op jit(solution)/shard_map/psum | solution.py:11
  68.0 1.5 gather_fusion
  69.5 1.7 convolution_bitcast_fusion.3
  71.2 1.5 copy.13
  72.8 1.3 scatter_fusion
  74.1 39.9 %all-reduce.8.cloned.1.call-done = f32[2,256,128]{2,1,0:T(8,128)} async-done(((f32[2,256,128]{2,1,0:T(8,128)}), f32[2,256,128]{2,1,0:T(8,128)}) %all-reduce.8.cloned.1.call-update) | async-done | bytes 262160 | tf_op jit(solution)/shard_map/psum | solution.py:50
  114.1 1.0 broadcast_multiply_fusion.1
  115.1 0.8 copy-done.2
  119.2 28.2 %reduce-scatter.3.cloned.1.call-done = f32[128,128]{1,0:T(8,128)} async-done(((f32[1024,128]{1,0:T(8,128)}), f32[128,128]{1,0:T(8,128)}) %reduce-scatter.3.cloned.1.call-update) | async-done | bytes 65552 | tf_op jit(solution)/shard_map/reduce_scatter | solution.py:55
  147.3 0.9 fusion.8
  148.2 14.2 %all_gather.7 = bf16[1024,128]{1,0:T(8,128)(2,1)S(1)} all-gather(bf16[128,128]{1,0:T(8,128)(2,1)S(1)} %fusion.8), channel_id=1, replica_groups=mesh['row'=4,'col'=8] {'col'}, dimensions={0}, use_global_device_ids=true | all-gather | bytes 294912 | tf_op jit(solution)/shard_map/all_gather | solution.py:35
  162.4 0.7 dynamic-slice_select_fusion
  164.6 1.3 scatter_fusion.3
  165.9 0.7 copy-done.3
  166.7 37.5 %all-reduce.10.cloned.1.call-done = bf16[2,256,128]{2,1,0:T(8,128)(2,1)} async-done(((bf16[2,256,128]{2,1,0:T(8,128)(2,1)}), bf16[2,256,128]{2,1,0:T(8,128)(2,1)}) %all-reduce.10.cloned.1.call-update) | async-done | bytes 131088 | tf_op jit(solution)/shard_map/psum | solution.py:11
  204.1 1.5 gather_fusion.2
  205.7 1.7 convolution_bitcast_fusion.1
  207.4 1.5 copy.17
  209.0 1.3 scatter_fusion.2
  210.3 39.6 %all-reduce.12.cloned.1.call-done = f32[2,256,128]{2,1,0:T(8,128)} async-done(((f32[2,256,128]{2,1,0:T(8,128)}), f32[2,256,128]{2,1,0:T(8,128)}) %all-reduce.12.cloned.1.call-update) | async-done | bytes 262160 | tf_op jit(solution)/shard_map/psum | solution.py:50
  249.9 1.0 broadcast_multiply_fusion
  250.9 0.8 copy-done.1
  251.8 31.3 %reduce-scatter.5.cloned.1.call-done = f32[128,128]{1,0:T(8,128)} async-done(((f32[1024,128]{1,0:T(8,128)}), f32[128,128]{1,0:T(8,128)}) %reduce-scatter.5.cloned.1.call-update) | async-done | bytes 65552 | tf_op jit(solution)/shard_map/reduce_scatter | solution.py:55
  283.1 0.9 divide_subtract_fusion
  283.9 0.9 fusion.10
  284.9 120.1 %all-reduce.14.cloned.1.call-done = f32[128,128]{1,0:T(8,128)} async-done(((f32[128,128]{1,0:T(8,128)}), f32[128,128]{1,0:T(8,128)}) %all-reduce.14.cloned.1.call-update) | async-done | bytes 65552 | tf_op jit(solution)/shard_map/psum | solution.py:68
  404.9 1.5 broadcast_multiply_fusion.2
  (50 shorter events, 5.0 us)
Async XLA Ops:
  7.2 19.6 %copy-start = (bf16[8,256,256]{2,1,0:T(8,128)(2,1)S(1)}, bf16[8,256,256]{2,1,0:T(8,128)(2,1)}, u32[]{:S(2)}) copy-start(bf16[8,256,256]{2,1,0:T(8,128)(2,1)} %param.6) | copy-start | bytes 3145732
  7.2 60.8 %all-reduce.6.cloned.1.call-start = ((), (), s32[]{:S(2)}) async-start(), calls=%async_computation.2 | async-start | bytes 262144 | tf_op jit(solution)/shard_map/psum | solution.py:11
  24.7 89.3 %all-reduce.8.cloned.1.call-start = ((), (), s32[]{:S(2)}) async-start(), calls=%async_computation.3 | async-start | bytes 524288 | tf_op jit(solution)/shard_map/psum | solution.py:50
  25.4 0.7 copy-start.9
  27.2 0.7 copy-start.10
  29.2 0.7 copy-start.4
  29.9 117.4 %reduce-scatter.3.cloned.1.call-start = ((), (), s32[]{:S(2)}) async-start(), calls=%async_computation.4 | async-start | bytes 589824 | tf_op jit(solution)/shard_map/reduce_scatter | solution.py:55
  115.1 0.8 copy-start.2
  115.1 0.9 copy-start.8
  115.1 32.2 %copy-start.5 = (f32[128,128]{1,0:T(8,128)S(1)}, f32[128,128]{1,0:T(8,128)}, u32[]{:S(2)}) copy-start(f32[128,128]{1,0:T(8,128)} %param.11) | copy-start | bytes 196612
  115.9 88.2 %all-reduce.10.cloned.1.call-start = ((), (), s32[]{:S(2)}) async-start(), calls=%async_computation.5 | async-start | bytes 262144 | tf_op jit(solution)/shard_map/psum | solution.py:11
  163.7 86.2 %all-reduce.12.cloned.1.call-start = ((), (), s32[]{:S(2)}) async-start(), calls=%async_computation.6 | async-start | bytes 524288 | tf_op jit(solution)/shard_map/psum | solution.py:50
  165.9 0.7 copy-start.3
  166.6 116.4 %reduce-scatter.5.cloned.1.call-start = ((), (), s32[]{:S(2)}) async-start(), calls=%async_computation.7 | async-start | bytes 589824 | tf_op jit(solution)/shard_map/reduce_scatter | solution.py:55
  250.9 0.8 copy-start.1
  250.9 32.2 %copy-start.7 = (f32[128,128]{1,0:T(8,128)S(1)}, f32[128,128]{1,0:T(8,128)}, u32[]{:S(2)}) copy-start(f32[128,128]{1,0:T(8,128)} %reduce-scatter.3.cloned.1.call-done) | copy-start | bytes 196612
  251.7 153.2 %all-reduce.14.cloned.1.call-start = ((), (), s32[]{:S(2)}) async-start(), calls=%async_computation.8 | async-start | bytes 131072 | tf_op jit(solution)/shard_map/psum | solution.py:68
  283.9 0.9 copy-start.6
Sparse Core Ops, SparseCore 0:
  24.9 43.0 all-reduce.5
  71.1 42.9 all-reduce.7
  116.4 30.9 reduce-scatter.2
  163.8 40.2 all-reduce.9
  206.9 42.9 all-reduce.11
  252.1 30.9 reduce-scatter.4
  289.2 115.6 all-reduce.13
where the time goes:
time: 415 us; the launch traced here: 413 us
  waiting for transfers between devices  335 us (81%)
  blocking collectives  30.1 us (7%)
  between operations  17.7 us (4%)
  local copies, waits for them, and re-layouts  12.8 us (3%)
  other arithmetic  12.8 us (3%)
  matrix products  5.16 us (1%)
    psum x1, waiting for transfers between devices, on_device(): gram_total = lax.psum(gram_local, ('row', 'col'))  120 us
    psum x2, waiting for transfers between devices, apply_hamiltonian(): column_total = lax.psum(col_part, 'row')  79.5 us
    psum x2, waiting for transfers between devices, spread(): return lax.psum(block, axis)  75.4 us
    reduce_scatter x2, waiting for transfers between devices, apply_hamiltonian(): return lax.psum_scatter(row_part, 'col', scatter_dimension=0, tiled=True)  59.5 us
    all_gather x2, blocking collectives, apply_hamiltonian(): row_panel = lax.all_gather(vector_panel, 'col', axis=0, tiled=True)  30.1 us
  transfers between devices with their start and end apart: 7, of which 7 were waited for; matrix products, arithmetic and copies ran while one was open for 4% of the time, Pallas kernels for 0%

commit v1 on v0

v1 whole, which is shorter than its diff:
```python
import functools

import jax
import jax.numpy as jnp
from jax import lax
from jax.experimental import pallas as pl
from jax.experimental.pallas import tpu as pltpu
from jax.sharding import PartitionSpec as P

BLK_COL = 2
GRAM_ROWS = 8
MESH = pl.DeviceIdType.MESH


def body(
    n_row,
    n_col,
    tile_rows,
    tile_cols,
    tile_count,
    bounds,
    tiles_hbm,
    vectors,
    filtered,
    gram,
    tiles,
    panel_h,
    panel_t,
    piece,
    panel,
    fwd,
    bwd,
    fwd_send,
    bwd_send,
    landed,
    current,
    gram_part,
    gram_land,
    gram_sum,
    gram_all,
    tile_sem,
    ga_send,
    ga_recv,
    sc_send,
    sc_recv,
    gram_sems,
):
    slots, size, _ = tiles_hbm.shape
    share, width = vectors.shape
    ratio = n_col // n_row
    group = share * n_col
    blocks = group // size
    column = BLK_COL * size
    owners = column // share
    n_dev = n_row * n_col
    reducers = width // GRAM_ROWS
    stride = n_dev // reducers
    row, col = lax.axis_index("row"), lax.axis_index("col")
    me = row * n_col + col
    live = row * ratio <= col
    diagonal = row == col // ratio
    first_live = row * ratio
    column_of_mine = row * ratio + col // owners
    place_in_column = col % owners
    column_base = jnp.where(diagonal, (col % ratio) * owners, n_col)

    def loop(low, high, step):
        def run(i, carry):
            step(i)
            return carry

        lax.fori_loop(low, high, run, 0)

    def device(index):
        return (index // n_col, index % n_col)

    tile_copy = pltpu.make_async_copy(tiles_hbm, tiles.at[pl.ds(0, slots)], tile_sem)
    tile_copy.start()

    barrier = pltpu.get_barrier_semaphore()

    def greet(i):
        pl.semaphore_signal(
            barrier, inc=1, device_id=device(lax.rem(me + i, n_dev)), device_id_type=MESH
        )

    loop(1, n_dev, greet)

    center = (bounds[1] + bounds[0]) * 0.5
    halfwidth = (bounds[1] - bounds[0]) * 0.5
    piece[0] = vectors[...].astype(jnp.bfloat16)
    tiles[slots] = jnp.zeros((size, size), jnp.bfloat16)
    pl.semaphore_wait(barrier, n_dev - 1)

    def gather_row(k, other):
        return pltpu.make_async_remote_copy(
            src_ref=piece.at[k],
            dst_ref=panel.at[k, col],
            send_sem=ga_send.at[k, other],
            recv_sem=ga_recv.at[k, col],
            device_id=(row, other),
            device_id_type=MESH,
        )

    def gather_column(k, other):
        return pltpu.make_async_remote_copy(
            src_ref=piece.at[k],
            dst_ref=panel.at[k, n_col + place_in_column],
            send_sem=ga_send.at[k, n_col + other],
            recv_sem=ga_recv.at[k, n_col + place_in_column],
            device_id=(other, column_of_mine),
            device_id_type=MESH,
        )

    def gather_landed(k, slot):
        return pltpu.make_async_remote_copy(
            src_ref=piece.at[k],
            dst_ref=panel.at[k, slot],
            send_sem=ga_send.at[k, 0],
            recv_sem=ga_recv.at[k, slot],
            device_id=(row, lax.rem(col + 1, n_col)),
            device_id_type=MESH,
        )

    def scatter_row(k, other):
        return pltpu.make_async_remote_copy(
            src_ref=fwd_send.at[k, other],
            dst_ref=landed.at[k, col],
            send_sem=sc_send.at[k, other],
            recv_sem=sc_recv.at[k, col],
            device_id=(row, other),
            device_id_type=MESH,
        )

    def scatter_column(k, j):
        return pltpu.make_async_remote_copy(
            src_ref=bwd_send.at[k, j],
            dst_ref=landed.at[k, n_col + row],
            send_sem=sc_send.at[k, n_col + j],
            recv_sem=sc_recv.at[k, n_col + row],
            device_id=(col // ratio, (col % ratio) * owners + j),
            device_id_type=MESH,
        )

    def scatter_landed(k, slot):
        return pltpu.make_async_remote_copy(
            src_ref=piece.at[k],
            dst_ref=landed.at[k, slot],
            send_sem=sc_send.at[k, 0],
            recv_sem=sc_recv.at[k, slot],
            device_id=(row, lax.rem(col + 1, n_col)),
            device_id_type=MESH,
        )

    def not_me(other, action):
        @pl.when(other != col)
        def _():
            action()

    def start_gather(k):
        loop(first_live, n_col, lambda i: not_me(i, lambda: gather_row(k, i).start()))
        loop(0, row, lambda i: gather_column(k, i).start())

    def arrange():
        tile_copy.wait()
        for i in range(blocks):
            for j in range(BLK_COL):
                slot = jnp.int32(slots)
                for s in range(slots):
                    here = (tile_rows[s] == i) & (tile_cols[s] == j) & (s < tile_count[0])
                    slot = jnp.where(here, jnp.int32(s), slot)
                block = tiles[slot]
                panel_h[pl.ds(i * size, size), pl.ds(j * size, size)] = block
                panel_t[pl.ds(j * size, size), pl.ds(i * size, size)] = block.T

    def products(k):
        panel[k, col] = piece[k]
        loop(0, n_col, lambda i: not_me(i, lambda: gather_landed(k, i).wait_recv()))

        @pl.when(jnp.logical_not(diagonal))
        def _():
            loop(0, owners, lambda j: gather_landed(k, n_col + j).wait_recv())

        rows_in = panel[k, pl.ds(0, n_col)].reshape(group, width)
        cols_in = panel[k, pl.ds(column_base, owners)].reshape(column, width)
        for j in range(BLK_COL):
            part = jnp.dot(
                panel_t[pl.ds(j * size, size)], rows_in, preferred_element_type=jnp.float32
            )
            bwd[pl.ds(j * size, size)] = part
        for i in range(blocks):
            part = jnp.dot(
                panel_h[pl.ds(i * size, size)], cols_in, preferred_element_type=jnp.float32
            )
            fwd[pl.ds(i * size, size)] = part

        @pl.when(diagonal)
        def _():
            here = pl.ds(pl.multiple_of((col % ratio) * column, column), column)
            fwd[here] += bwd[...]

        fwd_send[k] = fwd[...].astype(jnp.bfloat16).reshape(n_col, share, width)
        loop(0, n_col, lambda i: not_me(i, lambda: scatter_row(k, i).start()))

        @pl.when(jnp.logical_not(diagonal))
        def _():
            bwd_send[k] = bwd[...].astype(jnp.bfloat16).reshape(owners, share, width)
            loop(0, owners, lambda j: scatter_column(k, j).start())

    def apply(k):
        @pl.when(live)
        def _():
            if k == 0:
                arrange()
            products(k)

        if k == 0:

            @pl.when(jnp.logical_not(live))
            def _():
                tile_copy.wait()

        @pl.when(live)
        def _():
            filtered[...] = fwd[pl.ds(pl.multiple_of(col * share, share), share)]

        @pl.when(jnp.logical_not(live))
        def _():
            filtered[...] = jnp.zeros_like(filtered)

        def add(slot):
            scatter_landed(k, slot).wait_recv()
            filtered[...] += landed[k, slot].astype(jnp.float32)

        loop(first_live, n_col, lambda i: not_me(i, lambda: add(i)))
        loop(0, row, lambda i: add(n_col + i))
        return filtered[...]

    def finish_sends(k):
        loop(first_live, n_col, lambda i: not_me(i, lambda: gather_row(k, i).wait_send()))
        loop(0, row, lambda i: gather_column(k, i).wait_send())

        @pl.when(live)
        def _():
            loop(0, n_col, lambda i: not_me(i, lambda: scatter_row(k, i).wait_send()))

            @pl.when(jnp.logical_not(diagonal))
            def _():
                loop(0, owners, lambda j: scatter_column(k, j).wait_send())

    start_gather(0)
    image = apply(0)
    first = (image - center * vectors[...]) / halfwidth
    current[...] = first
    piece[1] = first.astype(jnp.bfloat16)
    start_gather(1)
    image = apply(1)
    last = 2.0 * (image - center * current[...]) / halfwidth - vectors[...]
    filtered[...] = last

    part = lax.dot_general(
        last,
        last,
        (((0,), (0,)), ((), ())),
        precision=lax.Precision.HIGHEST,
        preferred_element_type=jnp.float32,
    )
    gram_part[...] = part.reshape(reducers, GRAM_ROWS, width)
    reduces = lax.rem(me, stride) == 0
    mine = me // stride

    def to_reducer(q):
        target = q * stride
        return pltpu.make_async_remote_copy(
            src_ref=gram_part.at[q],
            dst_ref=gram_land.at[lax.rem(me - target - 1 + n_dev, n_dev)],
            send_sem=gram_sems.at[0],
            recv_sem=gram_sems.at[1],
            device_id=device(target),
            device_id_type=MESH,
        )

    def from_reducer(i):
        return pltpu.make_async_remote_copy(
            src_ref=gram_sum,
            dst_ref=gram_all.at[mine],
            send_sem=gram_sems.at[2],
            recv_sem=gram_sems.at[3],
            device_id=device(lax.rem(me + i, n_dev)),
            device_id_type=MESH,
        )

    def wait_bytes(ref, sem):
        pltpu.make_async_copy(ref, ref, gram_sems.at[sem]).wait()

    def start_reduce(q):
        @pl.when(q * stride != me)
        def _():
            to_reducer(q).start()

    loop(0, reducers, start_reduce)
    finish_sends(0)

    @pl.when(reduces)
    def _():
        wait_bytes(gram_land, 1)
        total = gram_part[mine] + jnp.sum(gram_land[...], axis=0)
        gram_sum[...] = total / (share * n_dev)
        gram_all[mine] = gram_sum[...]
        loop(1, n_dev, lambda i: from_reducer(i).start())

    finish_sends(1)

    @pl.when(reduces)
    def _():
        wait_bytes(gram_part.at[pl.ds(0, reducers - 1)], 0)
        wait_bytes(gram_all.at[pl.ds(0, reducers - 1)], 3)
        wait_bytes(gram_land, 2)

    @pl.when(jnp.logical_not(reduces))
    def _():
        wait_bytes(gram_part, 0)
        wait_bytes(gram_all, 3)

    gram[...] = gram_all[...].reshape(width, width)


def on_device(n_row, n_col, tiles, tile_rows, tile_cols, tile_count, bounds, vectors):
    slots, size, _ = tiles.shape
    share, width = vectors.shape
    group = share * n_col
    column = BLK_COL * size
    owners = column // share
    reducers = width // GRAM_ROWS
    n_dev = n_row * n_col
    smem = pl.BlockSpec(memory_space=pltpu.SMEM)
    vmem = pl.BlockSpec(memory_space=pltpu.VMEM)
    half, full = jnp.bfloat16, jnp.float32
    return pl.pallas_call(
        functools.partial(body, n_row, n_col),
        out_shape=(
            jax.ShapeDtypeStruct((share, width), full),
            jax.ShapeDtypeStruct((width, width), full),
        ),
        in_specs=[smem, smem, smem, smem, pl.BlockSpec(memory_space=pl.ANY), vmem],
        out_specs=(vmem, vmem),
        scratch_shapes=[
            pltpu.VMEM((slots + 1, size, size), half),
            pltpu.VMEM((group, column), half),
            pltpu.VMEM((column, group), half),
            pltpu.VMEM((2, share, width), half),
            pltpu.VMEM((2, n_col + owners, share, width), half),
            pltpu.VMEM((group, width), full),
            pltpu.VMEM((column, width), full),
            pltpu.VMEM((2, n_col, share, width), half),
            pltpu.VMEM((2, owners, share, width), half),
            pltpu.VMEM((2, n_col + n_row, share, width), half),
            pltpu.VMEM((share, width), full),
            pltpu.VMEM((reducers, GRAM_ROWS, width), full),
            pltpu.VMEM((n_dev - 1, GRAM_ROWS, width), full),
            pltpu.VMEM((GRAM_ROWS, width), full),
            pltpu.VMEM((reducers, GRAM_ROWS, width), full),
            pltpu.SemaphoreType.DMA(()),
            pltpu.SemaphoreType.DMA((2, n_col + n_row)),
            pltpu.SemaphoreType.DMA((2, n_col + owners)),
            pltpu.SemaphoreType.DMA((2, n_col + owners)),
            pltpu.SemaphoreType.DMA((2, n_col + n_row)),
            pltpu.SemaphoreType.DMA((4,)),
        ],
        compiler_params=pltpu.CompilerParams(
            collective_id=0, has_side_effects=True, vmem_limit_bytes=48 * 1024 * 1024
        ),
    )(tile_rows, tile_cols, tile_count, bounds, tiles, vectors)


def solution(mesh):
    in_specs = (
        P(("row", "col"), None, None),
        P(("row", "col")),
        P(("row", "col")),
        P(("row", "col")),
        P(),
        P(("row", "col"), None),
    )
    out_specs = (P(("row", "col"), None), P())
    return jax.shard_map(
        functools.partial(on_device, mesh.shape["row"], mesh.shape["col"]),
        mesh=mesh,
        in_specs=in_specs,
        out_specs=out_specs,
        check_vma=False,
    )
```

time: 415 us -> 62.7 us (0.15)
  waiting for transfers between devices: 335 us -> 0 us
  Pallas kernels: 0 us -> 57.8 us
  blocking collectives: 30.1 us -> 0 us
  between operations: 17.7 us -> 1.37 us
  other arithmetic: 12.8 us -> 0 us
  local copies, waits for them, and re-layouts: 12.8 us -> 3.33 us
  matrix products: 5.16 us -> 0 us
    psum x5 -> x0, waiting for transfers between devices: 275 us -> none  [the longest x1 120 us: on_device(): gram_total = lax.psum(gram_local, ('row', 'col'))]
    reduce_scatter x2 -> x0, waiting for transfers between devices: 59.5 us -> none  [apply_hamiltonian(): return lax.psum_scatter(row_part, 'col', scatter_dimension=0, tiled=True)]
    pallas_call x0 -> x1, Pallas kernels: none -> 57.8 us  [on_device(): pl.pallas_call(functools.partial(body, n_row, n_col), out_shape=(jax.Shap...]
    all_gather x2 -> x0, blocking collectives: 30.1 us -> none  [apply_hamiltonian(): row_panel = lax.all_gather(vector_panel, 'col', axis=0, tiled=True)]
    scatter-add x4 -> x0, other arithmetic: 5.26 us -> none  [the longest x2 2.64 us: apply_hamiltonian(): row_part = start_rows.at[tile_rows].add(forward)]
    dot_general x5 -> x0, matrix products: 5.16 us -> none  [the longest x2 3.41 us: apply_hamiltonian(): jnp.einsum('tab,tbk->tak', tiles, masked_cols, preferred_element_type=jnp...]
    gather x4 -> x0, local copies, waits for them, and re-layouts: 4.39 us -> none  [the longest x2 3.1 us: apply_hamiltonian(): masked_cols = col_input[tile_cols] * live_mask[:, None, None]]
  transfers between devices with their start and end apart: 7 -> 0, of which waited for: 7 -> 0; matrix products, arithmetic and copies ran while one was open for 4% -> 0% of each run, Pallas kernels for 0% -> 0%
where the time goes in v1:
time: 62.7 us; the launch traced here: 62.5 us
  Pallas kernels  57.8 us (92%)
  local copies, waits for them, and re-layouts  3.33 us (5%)
  between operations  1.37 us (2%)
    pallas_call x1, Pallas kernels, on_device(): pl.pallas_call(functools.partial(body, n_row, n_col), out_shape=(jax.Shap...  57.8 us
    unnamed x12, local copies, waits for them, and re-layouts  3.33 us

profile of v1, /device:TPU:0, one launch (start us, length us, event | category | flops | bytes accessed | tf_op | source)
XLA Modules:
  0.0 62.5 jit_solution(14151003355956410518)
XLA Ops:
  0.6 0.0 copy-start.4
  0.6 0.0 copy-start.3
  0.7 0.0 copy-start.2
  1.3 0.0 copy-done.4
  1.3 0.0 copy-done.3
  1.4 0.0 copy-done.2
  1.4 0.0 copy-start
  1.4 1.2 %copy-done = bf16[8,256,256]{2,1,0:T(8,128)(2,1)S(1)} copy-done((bf16[8,256,256]{2,1,0:T(8,128)(2,1)S(1)}, bf16[8,256,256]{2,1,0:T(8,128)(2,1)}, u32[]{:S(2)}) %copy-start) | copy-done | bytes 1048600
  2.6 0.0 copy-start.1
  2.6 0.8 %copy-done.1 = f32[128,128]{1,0:T(8,128)S(1)} copy-done((f32[128,128]{1,0:T(8,128)S(1)}, f32[128,128]{1,0:T(8,128)}, u32[]{:S(2)}) %copy-start.1) | copy-done | bytes 65560
  3.4 57.8 %shard_map.77 = (f32[128,128]{1,0:T(8,128)S(1)}, f32[128,128]{1,0:T(8,128)S(1)}) custom-call(s32[8]{0:T(128)S(1)} %copy-done.2, s32[8]{0:T(128)S(1)} %copy-done.3, s32[1]{0:T(128)S(6)} %copy.10.tile_count, f32[2]{0:T(128)S(1)} %copy-done.4, bf16[8,256,256]{2,1,0:T(8,128)(2,1)S(1)} %copy-done, f32[128,128]{1,0:T(8,128)S(1)} %copy-done.1), custom_call_target="tpu_custom_call" | custom-call | tf_op jit(solution)/shard_map/pallas_call | solution.py:339
  61.2 0.6 %copy.11 = f32[128,128]{1,0:T(8,128)} copy(f32[128,128]{1,0:T(8,128)S(1)} %get-tuple-element.4) | data formatting | bytes 131072
  61.8 0.6 %copy.12 = f32[128,128]{1,0:T(8,128)} copy(f32[128,128]{1,0:T(8,128)S(1)} %get-tuple-element.5) | data formatting | bytes 131072
Async XLA Ops:
  0.6 0.7 %copy-start.4 = (f32[2]{0:T(128)S(1)}, f32[2]{0:T(128)}, u32[]{:S(2)}) copy-start(f32[2]{0:T(128)} %bounds.1) | copy-start | bytes 28
  0.6 0.7 %copy-start.3 = (s32[8]{0:T(128)S(1)}, s32[8]{0:T(128)}, u32[]{:S(2)}) copy-start(s32[8]{0:T(128)} %tile_cols.1) | copy-start | bytes 100
  0.7 0.7 %copy-start.2 = (s32[8]{0:T(128)S(1)}, s32[8]{0:T(128)}, u32[]{:S(2)}) copy-start(s32[8]{0:T(128)} %tile_rows.1) | copy-start | bytes 100
  1.4 1.2 %copy-start = (bf16[8,256,256]{2,1,0:T(8,128)(2,1)S(1)}, bf16[8,256,256]{2,1,0:T(8,128)(2,1)}, u32[]{:S(2)}) copy-start(bf16[8,256,256]{2,1,0:T(8,128)(2,1)} %tiles_hbm.1) | copy-start | bytes 3145732
  2.6 0.8 %copy-start.1 = (f32[128,128]{1,0:T(8,128)S(1)}, f32[128,128]{1,0:T(8,128)}, u32[]{:S(2)}) copy-start(f32[128,128]{1,0:T(8,128)} %vectors.1) | copy-start | bytes 196612

commit v2 on v1

v2 whole, which is shorter than its diff:
```python
import functools

import jax
import jax.numpy as jnp
from jax import lax
from jax.experimental import pallas as pl
from jax.experimental.pallas import tpu as pltpu
from jax.sharding import PartitionSpec as P

BLK_COL = 2
UNROLL = 8
MESH = pl.DeviceIdType.MESH


def body(
    n_row,
    n_col,
    rows_any,
    cols_any,
    count_any,
    bounds_any,
    tiles_any,
    vectors_any,
    filtered,
    gram,
    tile_rows,
    tile_cols,
    tile_count,
    bounds,
    tiles,
    vectors,
    panel_h,
    panel_t,
    piece,
    panel,
    fwd,
    bwd,
    swapped,
    fwd_send,
    bwd_send,
    landed,
    current,
    gram_part,
    gram_half,
    gram_z,
    gram_xy,
    in_sems,
    ga_send,
    ga_recv,
    swap_sems,
    sc_send,
    sc_recv,
    gram_sems,
):
    slots, size, _ = tiles_any.shape
    share, width = vectors.shape
    n_z = n_col // 2
    ratio = n_col // n_row
    group = share * n_col
    blocks = group // size
    column = BLK_COL * size
    owners = column // share
    pairs = size // (2 * share)
    n_dev = n_row * n_col
    row, col = lax.axis_index("row"), lax.axis_index("col")
    core = lax.rem(col, 2)
    zed = col // 2
    sibling = zed * 2 + 1 - core
    live = row * ratio <= col
    diagonal = row == col // ratio
    first_z = row * ratio // 2
    column_of_mine = row * ratio + col // owners
    place_in_column = lax.rem(col, owners)
    part_of_column = lax.rem(col, ratio)
    column_base = jnp.where(diagonal, part_of_column * owners, n_col)

    def loop(count, step):
        def run(i, carry):
            step(i)
            return carry

        if count <= UNROLL:
            for i in range(count):
                step(i)
        else:
            lax.fori_loop(0, count, run, 0)

    def when(condition, action):
        pl.when(condition)(action)

    def far_first(i):
        return jnp.where(zed < n_z // 2, n_z - 1 - i, i)

    def near_first(i):
        return jnp.where(zed < n_z // 2, i, n_z - 1 - i)

    def when_not(value, mine, action):
        @pl.when(value != mine)
        def _():
            action()

    inputs = [
        pltpu.make_async_copy(vectors_any, vectors, in_sems.at[0]),
        pltpu.make_async_copy(tiles_any, tiles.at[pl.ds(0, slots)], in_sems.at[1]),
        pltpu.make_async_copy(rows_any, tile_rows, in_sems.at[2]),
        pltpu.make_async_copy(cols_any, tile_cols, in_sems.at[3]),
        pltpu.make_async_copy(count_any, tile_count, in_sems.at[4]),
        pltpu.make_async_copy(bounds_any, bounds, in_sems.at[5]),
    ]
    for copy in inputs:
        copy.start()

    barrier = pltpu.get_barrier_semaphore()

    def greet(other_row, other_col):
        pl.semaphore_signal(
            barrier, inc=1, device_id=(other_row, other_col), device_id_type=MESH
        )

    greet(row, sibling)
    loop(n_z, lambda z: when_not(z, zed, lambda: greet(row, z * 2 + core)))
    loop(n_row, lambda i: when_not(i, row, lambda: greet(i, col)))
    loop(n_row, lambda i: when_not(i, row, lambda: greet(i, sibling)))
    loop(n_row, lambda i: when(i < row, lambda: greet(i, column_of_mine)))
    across = live & jnp.logical_not(diagonal)

    @pl.when(across)
    def _():
        loop(owners, lambda j: greet(col // ratio, part_of_column * owners + j))

    inputs[0].wait()
    piece[0] = vectors[...].astype(jnp.bfloat16)
    tiles[slots] = jnp.zeros((size, size), jnp.bfloat16)
    pl.semaphore_wait(
        barrier, n_z + 2 * (n_row - 1) + row + jnp.where(across, owners, 0)
    )

    def remote(src, dst, send, recv, other_row, other_col):
        return pltpu.make_async_remote_copy(
            src_ref=src,
            dst_ref=dst,
            send_sem=send,
            recv_sem=recv,
            device_id=(other_row, other_col),
            device_id_type=MESH,
        )

    def gather_row(k, z):
        other = z * 2 + core
        return remote(
            piece.at[k], panel.at[k, col], ga_send.at[k, other], ga_recv.at[k, col], row, other
        )

    def gather_pair(k, z):
        slot = z * 2 + core
        return remote(
            panel.at[k, slot],
            panel.at[k, slot],
            ga_send.at[k, z * 2 + 1 - core],
            ga_recv.at[k, slot],
            row,
            sibling,
        )

    def gather_column(k, other):
        slot = n_col + place_in_column
        return remote(
            piece.at[k],
            panel.at[k, slot],
            ga_send.at[k, n_col + other],
            ga_recv.at[k, slot],
            other,
            column_of_mine,
        )

    def gather_landed(k, slot):
        return remote(
            piece.at[k], panel.at[k, slot], ga_send.at[k, 0], ga_recv.at[k, slot], row, sibling
        )

    def swap(k, z):
        return remote(
            fwd.at[1 - core, z],
            swapped.at[k, z],
            swap_sems.at[k, 0, z],
            swap_sems.at[k, 1, z],
            row,
            sibling,
        )

    def scatter_row(k, z):
        return remote(
            fwd_send.at[k, z],
            landed.at[k, zed],
            sc_send.at[k, z],
            sc_recv.at[k, zed],
            row,
            z * 2 + core,
        )

    def scatter_column(k, j):
        return remote(
            bwd_send.at[k, lax.rem(j, 2), j // 2],
            landed.at[k, n_z + row],
            sc_send.at[k, n_z + j],
            sc_recv.at[k, n_z + row],
            col // ratio,
            part_of_column * owners + j,
        )

    def scatter_landed(k, slot):
        return remote(
            piece.at[k], landed.at[k, slot], sc_send.at[k, 0], sc_recv.at[k, slot], row, sibling
        )

    def start_gather(k):
        @pl.when(live)
        def _():
            panel[k, col] = piece[k]

        def to_row(i):
            z = far_first(i)
            when((z >= first_z) & (z != zed), lambda: gather_row(k, z).start())

        loop(n_z, to_row)
        loop(n_row, lambda i: when(i < row, lambda: gather_column(k, i).start()))
        when(live, lambda: gather_pair(k, zed).start())

    def arrange():
        for i in range(blocks):
            for j in range(BLK_COL):
                slot = jnp.int32(slots)
                for s in range(slots):
                    here = (tile_rows[s] == i) & (tile_cols[s] == j) & (s < tile_count[0])
                    slot = jnp.where(here, jnp.int32(s), slot)
                block = tiles[slot]
                panel_h[pl.ds(i * size, size), pl.ds(j * size, size)] = block
                panel_t[pl.ds(j * size, size), pl.ds(i * size, size)] = block.T

    def forward_pair(k, z):
        gather_landed(k, z * 2 + core).wait_recv()
        gather_pair(k, z).start()

    def backward(k):
        rows_in = panel[k, pl.ds(0, n_col)].reshape(group, width)
        for j in range(BLK_COL):
            part = jnp.dot(
                panel_t[pl.ds(j * size, size)], rows_in, preferred_element_type=jnp.float32
            ).reshape(pairs, 2, share, width)
            for half in range(2):
                bwd[half, pl.ds(j * pairs, pairs)] = part[:, half]

    def products(k):
        def forward(i):
            z = near_first(i)
            when_not(z, zed, lambda: forward_pair(k, z))

        def rest_of_row():
            loop(n_z, lambda z: gather_landed(k, z * 2 + 1 - core).wait_recv())

        loop(n_z, forward)

        @pl.when(across)
        def _():
            loop(owners, lambda j: gather_landed(k, n_col + j).wait_recv())

        @pl.when(diagonal)
        def _():
            rest_of_row()
            backward(k)

        cols_in = panel[k, pl.ds(column_base, owners)].reshape(column, width)
        for i in range(blocks):
            part = jnp.dot(
                panel_h[pl.ds(i * size, size)], cols_in, preferred_element_type=jnp.float32
            ).reshape(pairs, 2, share, width)
            for half in range(2):
                fwd[half, pl.ds(i * pairs, pairs)] = part[:, half]

        @pl.when(diagonal)
        def _():
            here = pl.ds(part_of_column * (owners // 2), owners // 2)
            for half in range(2):
                fwd[half, here] += bwd[half]

        loop(n_z, lambda i: swap(k, far_first(i)).start())

        @pl.when(across)
        def _():
            rest_of_row()
            backward(k)
            bwd_send[k] = bwd[...].astype(jnp.bfloat16)
            loop(owners, lambda j: scatter_column(k, j).start())

        def send(i):
            z = far_first(i)
            swap(k, z).wait_recv()

            @pl.when(z != zed)
            def _():
                fwd_send[k, z] = (fwd[core, z] + swapped[k, z]).astype(jnp.bfloat16)
                scatter_row(k, z).start()

        loop(n_z, send)
        filtered[...] = fwd[core, zed] + swapped[k, zed]
        loop(n_z, lambda z: swap(k, z).wait_send())

    def apply(k):
        if k == 0:
            for copy in inputs[1:]:
                copy.wait()

        @pl.when(live)
        def _():
            if k == 0:
                arrange()
            products(k)

        @pl.when(jnp.logical_not(live))
        def _():
            filtered[...] = jnp.zeros_like(filtered)

        def add(slot):
            scatter_landed(k, slot).wait_recv()
            filtered[...] += landed[k, slot].astype(jnp.float32)

        def add_row(i):
            z = near_first(i)
            when((z >= first_z) & (z != zed), lambda: add(z))

        loop(n_z, add_row)
        loop(n_row, lambda i: when(i < row, lambda: add(n_z + i)))
        return filtered[...]

    def finish_sends(k):
        def sent(z):
            when((z >= first_z) & (z != zed), lambda: gather_row(k, z).wait_send())

        loop(n_z, sent)
        loop(n_row, lambda i: when(i < row, lambda: gather_column(k, i).wait_send()))

        @pl.when(live)
        def _():
            loop(n_z, lambda z: gather_pair(k, z).wait_send())
            loop(n_z, lambda z: when_not(z, zed, lambda: scatter_row(k, z).wait_send()))

        @pl.when(across)
        def _():
            loop(owners, lambda j: scatter_column(k, j).wait_send())

    start_gather(0)
    image = apply(0)
    center = (bounds[1] + bounds[0]) * 0.5
    halfwidth = (bounds[1] - bounds[0]) * 0.5
    first = (image - center * vectors[...]) / halfwidth
    current[...] = first
    piece[1] = first.astype(jnp.bfloat16)
    start_gather(1)
    image = apply(1)
    last = 2.0 * (image - center * current[...]) / halfwidth - vectors[...]
    filtered[...] = last

    part = lax.dot_general(
        last,
        last,
        (((0,), (0,)), ((), ())),
        precision=lax.Precision.HIGHEST,
        preferred_element_type=jnp.float32,
    )
    height = width // 2
    gram_part[...] = part.reshape(2, height, width)

    def gram_swap():
        return remote(
            gram_part.at[1 - core], gram_half, gram_sems.at[0], gram_sems.at[1], row, sibling
        )

    def gram_row(z):
        return remote(
            gram_z.at[zed],
            gram_z.at[zed],
            gram_sems.at[2],
            gram_sems.at[3],
            row,
            z * 2 + core,
        )

    def gram_out(i, other):
        here = core * n_row + row
        return remote(
            gram_xy.at[here], gram_xy.at[here], gram_sems.at[4], gram_sems.at[5], i, other
        )

    def wait_bytes(ref, sem):
        pltpu.make_async_copy(ref, ref, gram_sems.at[sem]).wait()

    gram_swap().start()
    finish_sends(0)
    gram_swap().wait_recv()
    gram_z[zed] = gram_part[core] + gram_half[...]

    def to_row(i):
        z = far_first(i)
        when_not(z, zed, lambda: gram_row(z).start())

    loop(n_z, to_row)
    finish_sends(1)
    gram_swap().wait_send()
    wait_bytes(gram_z.at[pl.ds(0, n_z - 1)], 3)
    gram_xy[core * n_row + row] = jnp.sum(gram_z[...], axis=0)
    loop(n_row, lambda i: when_not(i, row, lambda: gram_out(i, col).start()))
    loop(n_row, lambda i: when_not(i, row, lambda: gram_out(i, sibling).start()))
    gram_out(row, sibling).start()
    wait_bytes(gram_z.at[pl.ds(0, n_z - 1)], 2)
    wait_bytes(gram_xy.at[pl.ds(0, 2 * n_row - 1)], 5)
    for half in range(2):
        total = jnp.sum(gram_xy[pl.ds(half * n_row, n_row)], axis=0)
        gram[pl.ds(half * height, height)] = total / (share * n_dev)
    wait_bytes(gram_xy.at[pl.ds(0, 2 * n_row - 1)], 4)


def on_device(n_row, n_col, tiles, tile_rows, tile_cols, tile_count, bounds, vectors):
    slots, size, _ = tiles.shape
    share, width = vectors.shape
    n_z = n_col // 2
    group = share * n_col
    column = BLK_COL * size
    owners = column // share
    height = width // 2
    hbm = pl.BlockSpec(memory_space=pl.ANY)
    vmem = pl.BlockSpec(memory_space=pltpu.VMEM)
    half, full = jnp.bfloat16, jnp.float32
    return pl.pallas_call(
        functools.partial(body, n_row, n_col),
        out_shape=(
            jax.ShapeDtypeStruct((share, width), full),
            jax.ShapeDtypeStruct((width, width), full),
        ),
        in_specs=[hbm] * 6,
        out_specs=(vmem, vmem),
        scratch_shapes=[
            pltpu.SMEM((slots,), jnp.int32),
            pltpu.SMEM((slots,), jnp.int32),
            pltpu.SMEM((1,), jnp.int32),
            pltpu.SMEM((2,), full),
            pltpu.VMEM((slots + 1, size, size), half),
            pltpu.VMEM((share, width), full),
            pltpu.VMEM((group, column), half),
            pltpu.VMEM((column, group), half),
            pltpu.VMEM((2, share, width), half),
            pltpu.VMEM((2, n_col + owners, share, width), half),
            pltpu.VMEM((2, n_z, share, width), full),
            pltpu.VMEM((2, owners // 2, share, width), full),
            pltpu.VMEM((2, n_z, share, width), full),
            pltpu.VMEM((2, n_z, share, width), half),
            pltpu.VMEM((2, 2, owners // 2, share, width), half),
            pltpu.VMEM((2, n_z + n_row, share, width), half),
            pltpu.VMEM((share, width), full),
            pltpu.VMEM((2, height, width), full),
            pltpu.VMEM((height, width), full),
            pltpu.VMEM((n_z, height, width), full),
            pltpu.VMEM((2 * n_row, height, width), full),
            pltpu.SemaphoreType.DMA((6,)),
            pltpu.SemaphoreType.DMA((2, n_col + n_row)),
            pltpu.SemaphoreType.DMA((2, n_col + owners)),
            pltpu.SemaphoreType.DMA((2, 2, n_z)),
            pltpu.SemaphoreType.DMA((2, n_z + owners)),
            pltpu.SemaphoreType.DMA((2, n_z + n_row)),
            pltpu.SemaphoreType.DMA((6,)),
        ],
        compiler_params=pltpu.CompilerParams(
            collective_id=0, has_side_effects=True, vmem_limit_bytes=58 * 1024 * 1024
        ),
    )(tile_rows, tile_cols, tile_count, bounds, tiles, vectors)


def solution(mesh):
    in_specs = (
        P(("row", "col"), None, None),
        P(("row", "col")),
        P(("row", "col")),
        P(("row", "col")),
        P(),
        P(("row", "col"), None),
    )
    out_specs = (P(("row", "col"), None), P())
    return jax.shard_map(
        functools.partial(on_device, mesh.shape["row"], mesh.shape["col"]),
        mesh=mesh,
        in_specs=in_specs,
        out_specs=out_specs,
        check_vma=False,
    )
```

time: 62.7 us -> 51 us (0.81)
  Pallas kernels: 57.8 us -> 47.4 us
  local copies, waits for them, and re-layouts: 3.33 us -> 2.14 us
    pallas_call x1, Pallas kernels: 57.8 us -> 47.4 us  [on_device(): pl.pallas_call(functools.partial(body, n_row, n_col), out_shape=(jax.Shap...]
    unnamed x12 -> x4, local copies, waits for them, and re-layouts: 3.33 us -> 2.14 us
where the time goes in v2:
time: 51 us; the launch traced here: 50.8 us
  Pallas kernels  47.4 us (93%)
  local copies, waits for them, and re-layouts  2.14 us (4%)
  between operations  1.29 us (3%)
    pallas_call x1, Pallas kernels, on_device(): pl.pallas_call(functools.partial(body, n_row, n_col), out_shape=(jax.Shap...  47.4 us
    unnamed x4, local copies, waits for them, and re-layouts  2.14 us

profile of v2, /device:TPU:0, one launch (start us, length us, event | category | flops | bytes accessed | tf_op | source)
XLA Modules:
  0.0 50.8 jit_solution(3195736206753264841)
XLA Ops:
  1.3 47.4 %shard_map.77 = (f32[128,128]{1,0:T(8,128)}, f32[128,128]{1,0:T(8,128)}) custom-call(s32[8]{0:T(128)} %rows_any.1, s32[8]{0:T(128)} %cols_any.1, s32[1]{0:T(128)S(6)} %copy.10.count_any, f32[2]{0:T(128)} %bounds_any.1, bf16[8,256,256]{2,1,0:T(8,128)(2,1)} %tiles_any.1, f32[128,128]{1,0:T(8,128)} %vectors_any.1), custom_call_target="tpu_custom_call" | custom-call | tf_op jit(solution)/shard_map/pallas_call | solution.py:433
  48.6 0.0 copy-start
  48.6 1.5 %copy.11 = f32[128,128]{1,0:T(8,128)} copy(f32[128,128]{1,0:T(8,128)} %get-tuple-element.4) | data formatting | bytes 131072
  50.2 0.0 copy-done
  50.2 0.6 %copy.12 = f32[128,128]{1,0:T(8,128)} copy(f32[128,128]{1,0:T(8,128)S(1)} %copy-done) | data formatting | bytes 131072
Async XLA Ops:
  48.6 1.5 %copy-start = (f32[128,128]{1,0:T(8,128)S(1)}, f32[128,128]{1,0:T(8,128)}, u32[]{:S(2)}) copy-start(f32[128,128]{1,0:T(8,128)} %get-tuple-element.5) | copy-start | bytes 196612

commit v3 on v2

--- a/solution.py
+++ b/solution.py
@@ -21,8 +21,7 @@
     bounds_any,
     tiles_any,
     vectors_any,
-    filtered,
-    gram,
+    out,
     tile_rows,
     tile_cols,
     tile_count,
@@ -54,6 +53,8 @@
 ):
     slots, size, _ = tiles_any.shape
     share, width = vectors.shape
+    filtered = out.at[pl.ds(0, share)]
+    gram = out.at[pl.ds(share, width)]
     n_z = n_col // 2
     ratio = n_col // n_row
     group = share * n_col
@@ -397,7 +398,7 @@
     gram_swap().start()
     finish_sends(0)
     gram_swap().wait_recv()
-    gram_z[zed] = gram_part[core] + gram_half[...]
+    gram_z[zed] = (gram_part[core] + gram_half[...]).astype(jnp.bfloat16)
 
     def to_row(i):
         z = far_first(i)
@@ -407,14 +408,16 @@
     finish_sends(1)
     gram_swap().wait_send()
     wait_bytes(gram_z.at[pl.ds(0, n_z - 1)], 3)
-    gram_xy[core * n_row + row] = jnp.sum(gram_z[...], axis=0)
+    gram_xy[core * n_row + row] = jnp.sum(gram_z[...].astype(jnp.float32), axis=0).astype(
+        jnp.bfloat16
+    )
     loop(n_row, lambda i: when_not(i, row, lambda: gram_out(i, col).start()))
     loop(n_row, lambda i: when_not(i, row, lambda: gram_out(i, sibling).start()))
     gram_out(row, sibling).start()
     wait_bytes(gram_z.at[pl.ds(0, n_z - 1)], 2)
     wait_bytes(gram_xy.at[pl.ds(0, 2 * n_row - 1)], 5)
     for half in range(2):
-        total = jnp.sum(gram_xy[pl.ds(half * n_row, n_row)], axis=0)
+        total = jnp.sum(gram_xy[pl.ds(half * n_row, n_row)].astype(jnp.float32), axis=0)
         gram[pl.ds(half * height, height)] = total / (share * n_dev)
     wait_bytes(gram_xy.at[pl.ds(0, 2 * n_row - 1)], 4)
 
@@ -430,14 +433,11 @@
     hbm = pl.BlockSpec(memory_space=pl.ANY)
     vmem = pl.BlockSpec(memory_space=pltpu.VMEM)
     half, full = jnp.bfloat16, jnp.float32
-    return pl.pallas_call(
+    both = pl.pallas_call(
         functools.partial(body, n_row, n_col),
-        out_shape=(
-            jax.ShapeDtypeStruct((share, width), full),
-            jax.ShapeDtypeStruct((width, width), full),
-        ),
-        in_specs=[hbm] * 6,
-        out_specs=(vmem, vmem),
+        out_shape=jax.ShapeDtypeStruct((share + width, width), full),
+        in_specs=[pl.BlockSpec(memory_space=pltpu.HBM)] * 6,
+        out_specs=vmem,
         scratch_shapes=[
             pltpu.SMEM((slots,), jnp.int32),
             pltpu.SMEM((slots,), jnp.int32),
@@ -458,8 +458,8 @@
             pltpu.VMEM((share, width), full),
             pltpu.VMEM((2, height, width), full),
             pltpu.VMEM((height, width), full),
-            pltpu.VMEM((n_z, height, width), full),
-            pltpu.VMEM((2 * n_row, height, width), full),
+            pltpu.VMEM((n_z, height, width), half),
+            pltpu.VMEM((2 * n_row, height, width), half),
             pltpu.SemaphoreType.DMA((6,)),
             pltpu.SemaphoreType.DMA((2, n_col + n_row)),
             pltpu.SemaphoreType.DMA((2, n_col + owners)),
@@ -472,6 +472,7 @@
             collective_id=0, has_side_effects=True, vmem_limit_bytes=58 * 1024 * 1024
         ),
     )(tile_rows, tile_cols, tile_count, bounds, tiles, vectors)
+    return both[:share], both[share:]
 
 
 def solution(mesh):

time: 51 us -> 49.1 us (0.963)
  Pallas kernels: 47.4 us -> 46.1 us
  local copies, waits for them, and re-layouts: 2.14 us -> 1.53 us
    unnamed x4 -> x0, local copies, waits for them, and re-layouts: 2.14 us -> none
    slice x0 -> x1, local copies, waits for them, and re-layouts: none -> 1.53 us  [on_device(): return (both[:share], both[share:])]
    pallas_call x1, Pallas kernels: 47.4 us -> 46.1 us  [on_device(): pl.pallas_call(functools.partial(body, n_row, n_col), out_shape=jax.Shape...]
where the time goes in v3:
time: 49.1 us; the launch traced here: 48.9 us
  Pallas kernels  46.1 us (94%)
  local copies, waits for them, and re-layouts  1.53 us (3%)
  between operations  1.28 us (3%)
    pallas_call x1, Pallas kernels, on_device(): pl.pallas_call(functools.partial(body, n_row, n_col), out_shape=jax.Shape...  46.1 us
    slice x1, local copies, waits for them, and re-layouts, on_device(): return (both[:share], both[share:])  1.53 us

profile of v3, /device:TPU:0, one launch (start us, length us, event | category | flops | bytes accessed | tf_op | source)
XLA Modules:
  0.0 48.9 jit_solution(16644241405154750955)
XLA Ops:
  1.3 46.1 %shard_map.77 = f32[256,128]{1,0:T(8,128)} custom-call(s32[8]{0:T(128)} %rows_any.1, s32[8]{0:T(128)} %cols_any.1, s32[1]{0:T(128)S(6)} %copy.8.count_any, f32[2]{0:T(128)} %bounds_any.1, bf16[8,256,256]{2,1,0:T(8,128)(2,1)} %tiles_any.1, f32[128,128]{1,0:T(8,128)} %vectors_any.1), custom_call_target="tpu_custom_call" | custom-call | tf_op jit(solution)/shard_map/pallas_call | solution.py:436
  47.3 1.5 %fusion = (f32[128,128]{1,0:T(8,128)}, f32[128,128]{1,0:T(8,128)}) fusion(f32[256,128]{1,0:T(8,128)} %shard_map.77), kind=kLoop, calls=%fused_computation | loop fusion | bytes 262144 | tf_op jit(solution)/shard_map/slice | solution.py:475

commit v4 on v3

--- a/solution.py
+++ b/solution.py
@@ -118,17 +118,22 @@
             barrier, inc=1, device_id=(other_row, other_col), device_id_type=MESH
         )
 
-    greet(row, sibling)
-    loop(n_z, lambda z: when_not(z, zed, lambda: greet(row, z * 2 + core)))
-    loop(n_row, lambda i: when_not(i, row, lambda: greet(i, col)))
-    loop(n_row, lambda i: when_not(i, row, lambda: greet(i, sibling)))
+    across = live & jnp.logical_not(diagonal)
+
+    def greet_row(i):
+        z = far_first(i)
+        when_not(z, zed, lambda: greet(row, z * 2 + core))
+
+    loop(n_z, greet_row)
     loop(n_row, lambda i: when(i < row, lambda: greet(i, column_of_mine)))
-    across = live & jnp.logical_not(diagonal)
 
     @pl.when(across)
     def _():
         loop(owners, lambda j: greet(col // ratio, part_of_column * owners + j))
 
+    loop(n_row, lambda i: when_not(i, row, lambda: greet(i, col)))
+    loop(n_row, lambda i: when_not(i, row, lambda: greet(i, sibling)))
+    greet(row, sibling)
     inputs[0].wait()
     piece[0] = vectors[...].astype(jnp.bfloat16)
     tiles[slots] = jnp.zeros((size, size), jnp.bfloat16)

time: 49.1 us -> 49 us (level)
  no operation moved by 1% of the time
where the time goes in v4:
time: 49 us; the launch traced here: 48.8 us
  Pallas kernels  46 us (94%)
  local copies, waits for them, and re-layouts  1.53 us (3%)
  between operations  1.28 us (3%)
    pallas_call x1, Pallas kernels, on_device(): pl.pallas_call(functools.partial(body, n_row, n_col), out_shape=jax.Shape...  46 us
    slice x1, local copies, waits for them, and re-layouts, on_device(): return (both[:share], both[share:])  1.53 us

profile of v4, /device:TPU:0, one launch (start us, length us, event | category | flops | bytes accessed | tf_op | source)
XLA Modules:
  0.0 48.8 jit_solution(2517634769851909848)
XLA Ops:
  1.3 46.0 %shard_map.77 = f32[256,128]{1,0:T(8,128)} custom-call(s32[8]{0:T(128)} %rows_any.1, s32[8]{0:T(128)} %cols_any.1, s32[1]{0:T(128)S(6)} %copy.8.count_any, f32[2]{0:T(128)} %bounds_any.1, bf16[8,256,256]{2,1,0:T(8,128)(2,1)} %tiles_any.1, f32[128,128]{1,0:T(8,128)} %vectors_any.1), custom_call_target="tpu_custom_call" | custom-call | tf_op jit(solution)/shard_map/pallas_call | solution.py:441
  47.3 1.5 %fusion = (f32[128,128]{1,0:T(8,128)}, f32[128,128]{1,0:T(8,128)}) fusion(f32[256,128]{1,0:T(8,128)} %shard_map.77), kind=kLoop, calls=%fused_computation | loop fusion | bytes 262144 | tf_op jit(solution)/shard_map/slice | solution.py:480
